TPU v7x, 32 devices: a whole 2x2x4 slice. The times are simulated.
32 devices in a mesh: grp: 2 (over x), space: 16 (over z, y, core).
Axes of the slice: x: 2, y: 2, z: 4, core: 2. Of those that a mesh axis runs over, the one named last changes fastest.
Arguments:
- right_side: float32 [64, 32, 4096], P(None, None, ('grp', 'space')), parts along dimension 2, may hold values from -36 to 36
- diag_tiles: bfloat16 [64, 64, 4096], P(None, None, ('grp', 'space')), parts along dimension 2, may hold values from -0.5 to 4.5, as said below
- off_tiles: bfloat16 [15, 64, 64, 4096], P(None, None, None, ('grp', 'space')), parts along dimension 3, may hold values from -0.1875 to 0.1875
- neighbours: int32 [15, 4096], P(None, ('grp', 'space')), parts along dimension 1, may hold values from -192 to 2046, as said below
Outputs:
- solution: float32 [64, 32, 4096], P(None, None, ('grp', 'space')), parts along dimension 2
- residual: float32 [64, 32, 4096], P(None, None, ('grp', 'space')), parts along dimension 2
There are 2 independent parts, one for each index of `grp`. A program takes and returns all parts, laid end to end along the dimension named above; each array names one. Nothing has to cross between parts.
Inputs may be any that keep to these rules, and one draw needn't show every extreme that they name: `neighbours`: the 15 ids of one block i differ and lie from i - 192 to i - 1; ids below 0 name no block and add nothing. `diag_tiles`: diagonal tiles have positive diagonals of 1.2 to 4 and smaller entries off them.
All inputs are finite; a program needn't handle non-finite values.
Results may differ from a plain program's by a relative error of at most 0.0068.
Values may be sent and summed in bfloat16 or wider, within the bound.
A program may use at most 192 MiB of HBM per device.

v0:
```python
import jax
import jax.numpy as jnp
from jax import lax
from jax.sharding import PartitionSpec as P


def from_behind(value, axis, steps):
    count = lax.axis_size(axis)
    first, last = (max(0, -steps), min(count, count - steps))
    return lax.ppermute(value, axis, [(source, source + steps) for source in range(first, last)])


def on_device(right_side, diag_tiles, off_tiles, neighbours):
    highest = lax.Precision.HIGHEST
    blocks = right_side.shape[2]
    extra = blocks // 2
    device = lax.axis_index("space")
    norm_local = jnp.sum(right_side * right_side, axis=(0, 2))
    norm = lax.psum(norm_local, "space")
    rounded = right_side.astype(jnp.bfloat16)
    earlier = from_behind(rounded, "space", 1)
    oldest = from_behind(rounded[:, :, blocks - extra :], "space", 2)
    table = jnp.concatenate([oldest, earlier, rounded], axis=2)
    total = 2 * blocks + extra
    offset = device * blocks - blocks - extra
    local_ids = neighbours - offset
    columns = jnp.arange(total, dtype=jnp.int32)
    selector = local_ids[:, :, None] == columns[None, None, :]
    picker = selector.astype(jnp.bfloat16)
    picked = jnp.einsum("lrt,nit->lrni", table, picker, preferred_element_type=jnp.float32).astype(
        jnp.bfloat16
    )
    image = jnp.einsum("lki,kri->lri", diag_tiles, rounded, preferred_element_type=jnp.float32)
    image = image + jnp.einsum(
        "nlki,krni->lri", off_tiles, picked, preferred_element_type=jnp.float32
    )
    image_rounded = image.astype(jnp.bfloat16)
    own_terms = jnp.einsum(
        "kli,kri->lri", diag_tiles, image_rounded, preferred_element_type=jnp.float32
    )
    coupled = jnp.einsum(
        "nlki,lri->krni", off_tiles, image_rounded, preferred_element_type=jnp.float32
    )
    spreader = selector.astype(jnp.float32)
    collected = jnp.einsum(
        "krni,nit->krt", coupled, spreader, precision=highest, preferred_element_type=jnp.float32
    )
    for_oldest = collected[:, :, :extra]
    for_earlier = collected[:, :, extra : extra + blocks]
    own_terms = own_terms + collected[:, :, extra + blocks :]
    from_next = from_behind(for_earlier.astype(jnp.bfloat16), "space", -1).astype(for_earlier.dtype)
    from_after = from_behind(for_oldest.astype(jnp.bfloat16), "space", -2).astype(for_oldest.dtype)
    product = own_terms + from_next
    product = product.at[:, :, blocks - extra :].add(from_after)
    curve_local = jnp.sum(image * image_rounded.astype(jnp.float32), axis=(0, 2))
    curve = lax.psum(curve_local, "space")
    step_size = (norm / curve)[None, :, None]
    solution = step_size * right_side
    residual = right_side - step_size * product
    return (solution, residual)


def solution(mesh):
    placed = (
        P(None, None, ("grp", "space")),
        P(None, None, ("grp", "space")),
        P(None, None, None, ("grp", "space")),
        P(None, ("grp", "space")),
    )
    return jax.shard_map(
        on_device,
        mesh=mesh,
        in_specs=placed,
        out_specs=(P(None, None, ("grp", "space")), P(None, None, ("grp", "space"))),
        check_vma=False,
    )
```

profile of v0, /device:TPU:0, one launch (start us, length us, event | category | flops | bytes accessed | tf_op | source)
XLA Modules:
  0.0 267.0 jit_solution(1006299897619427484)
XLA Ops:
  2.5 3.2 %collective-permute-start.1 = (bf16[64,32,128]{2,1,0:T(8,128)(2,1)S(1)}, bf16[64,32,128]{2,1,0:T(8,128)(2,1)}, u32[]{:S(2)}, u32[]{:S(2)}) collective-permute-start(bf16[64,32,128]{2,1,0:T(8,128)(2,1)S(1)} %get-tuple-element.22), channel_id=1, source_target_pairs={{0,1},{1,2},{2,3},{3,4},{4,5},{5,6},{6,7},{7,8},{8,9},{9,10},{10,1... | collective-permute-start | bytes 1572872 | tf_op jit(solution)/shard_map/ppermute | solution.py:10
  5.9 4.5 %collective-permute-start = (bf16[64,32,64]{2,1,0:T(8,128)(2,1)S(1)}, bf16[64,32,64]{2,1,0:T(8,128)(2,1)}, u32[]{:S(2)}, u32[]{:S(2)}) collective-permute-start(bf16[64,32,64]{2,1,0:T(8,128)(2,1)S(1)} %slice.43), channel_id=1, source_target_pairs={{0,2},{1,3},{2,4},{3,5},{4,6},{5,7},{6,8},{7,9},{8,10},{9,11},{10,... | collective-permute-start | bytes 786440 | tf_op jit(solution)/shard_map/ppermute | solution.py:10
  10.3 2.6 copy.16
  12.9 3.9 %copy.17 = bf16[64,64,128]{1,0,2:T(8,128)(2,1)S(1)} copy(bf16[64,64,128]{2,1,0:T(8,128)(2,1)} %param.7) | data formatting | bytes 2097152 | tf_op args[1]
  16.8 3.7 %fusion.32 = f32[128,32,64]{2,1,0:T(8,128)} fusion(bf16[64,32,128]{0,1,2:T(8,128)(2,1)} %copy.16, bf16[64,64,128]{1,0,2:T(8,128)(2,1)S(1)} %copy.17), kind=kOutput, calls=%fused_computation.34 | convolution fusion | flops 33554432 | bytes 2621440 | tf_op jit(solution)/shard_map/lki,kri->lri/dot_general | solution.py:33
  20.6 43.3 %copy.18 = bf16[15,64,64,128]{2,1,0,3:T(8,128)(2,1)} copy(bf16[15,64,64,128]{3,2,1,0:T(8,128)(2,1)} %param.8) | data formatting | bytes 31457280 | tf_op args[2]
  63.9 8.1 %fusion.6 = bf16[64,32,15,128]{3,1,2,0:T(8,128)(2,1)} fusion(bf16[64,32,128]{2,1,0:T(8,128)(2,1)S(1)} %get-tuple-element.22, bf16[64,32,128]{2,1,0:T(8,128)(2,1)} %collective-permute-done.1, bf16[64,32,64]{2,1,0:T(8,128)(2,1)} %collective-permute-done, s32[15,128]{1,0:T(8,128)S(1)} %broadcast_subtract_fusion), kind=kOutput, calls=%fused_computation.6 | convolution fusion | flops 2521128960 | bytes 9182720 | tf_op jit(solution)/shard_map/lrt,nit->lrni/dot_general | solution.py:30
  72.0 27.5 %copy.29 = bf16[64,32,15,128]{0,1,2,3:T(8,128)(2,1)} copy(bf16[64,32,15,128]{3,1,2,0:T(8,128)(2,1)} %fusion.6) | data formatting | bytes 15728640 | tf_op jit(solution)/shard_map/lrt,nit->lrni/dot_general | solution.py:30
  99.4 18.2 %fusion.9 = (f32[32]{0:T(128)S(1)}, bf16[128,32,64]{2,1,0:T(8,128)(2,1)S(1)}) fusion(f32[128,32,64]{2,1,0:T(8,128)} %fusion.32, bf16[64,32,15,128]{0,1,2,3:T(8,128)(2,1)} %copy.29, bf16[15,64,64,128]{2,1,0,3:T(8,128)(2,1)} %copy.18), kind=kOutput, calls=%fused_computation.11 | convolution fusion | flops 504889312 | bytes 25165952 | tf_op jit(solution)/shard_map/nlki,krni->lri/dot_general | solution.py:34
  117.6 23.3 %fusion.24 = f32[128,32,15,64]{3,1,2,0:T(8,128)} fusion(bf16[15,64,64,128]{2,1,0,3:T(8,128)(2,1)} %copy.18, bf16[128,32,64]{2,1,0:T(8,128)(2,1)S(1)} %get-tuple-element.25), kind=kOutput, calls=%fused_computation.24 | convolution fusion | flops 503316480 | bytes 31981568 | tf_op jit(solution)/shard_map/nlki,lri->krni/dot_general | solution.py:41
  140.9 27.7 %copy.32 = f32[128,32,15,64]{0,1,2,3:T(8,128)} copy(f32[128,32,15,64]{3,1,2,0:T(8,128)} %fusion.24) | data formatting | bytes 31457280 | tf_op jit(solution)/shard_map/nlki,lri->krni/dot_general | solution.py:41
  168.6 16.7 %fusion.10 = f32[64,32,320]{2,1,0:T(8,128)} fusion(f32[128,32,15,64]{0,1,2,3:T(8,128)} %copy.32, s32[15,128]{1,0:T(8,128)S(1)} %broadcast_subtract_fusion), kind=kOutput, calls=%fused_computation.14 | convolution fusion | flops 15100108800 | bytes 18357760 | tf_op jit(solution)/shard_map/krni,nit->krt/dot_general | solution.py:45
  185.3 7.2 %copy.21 = f32[64,32,320]{0,1,2:T(8,128)} copy(f32[64,32,320]{2,1,0:T(8,128)} %fusion.10) | data formatting | bytes 5242880 | tf_op jit(solution)/shard_map/krni,nit->krt/dot_general | solution.py:45
  192.5 3.1 %convert.4 = bf16[64,32,320]{0,1,2:T(8,128)(2,1)S(1)} convert(f32[64,32,320]{0,1,2:T(8,128)} %copy.21) | non-fusion elementwise | flops 655360 | bytes 3932160 | tf_op jit(solution)/shard_map/convert.1
  198.2 3.6 %copy.23 = bf16[64,32,128]{2,1,0:T(8,128)(2,1)} copy(bf16[64,32,128]{0,1,2:T(8,128)(2,1)} %slice.45) | data formatting | bytes 1048576 | tf_op jit(solution)/shard_map/slice | solution.py:49
  203.0 4.1 %copy.19 = f32[64,32,128]{0,1,2:T(8,128)} copy(f32[64,32,128]{2,1,0:T(8,128)} %param.6) | data formatting | bytes 2097152 | tf_op args[0]
  207.2 1.9 slice.47
  210.3 38.7 %all-reduce = (f32[32]{0:T(128)S(1)}, f32[32]{0:T(128)S(1)}) all-reduce(f32[32]{0:T(128)S(1)} %get-tuple-element.23, f32[32]{0:T(128)S(1)} %get-tuple-element.24), channel_id=1, replica_groups=mesh['grp'=2,'space'=16] {'space'}, use_global_device_ids=true, to_apply=%region_1.0 | all-reduce | flops 64 | bytes 512 | tf_op jit(solution)/shard_map/psum | solution.py:19
  249.1 2.0 fusion.30
  251.1 2.8 %copy.24 = bf16[64,32,128]{0,1,2:T(8,128)(2,1)S(1)} copy(bf16[64,32,128]{2,1,0:T(8,128)(2,1)} %collective-permute-done.2) | data formatting | bytes 1048576 | tf_op jit(solution)/shard_map/ppermute | solution.py:10
  253.9 2.8 %fusion.8 = f32[64,32,128]{0,1,2:T(8,128)S(1)} fusion(f32[64,32,320]{0,1,2:T(8,128)} %copy.21, f32[128,32,64]{2,1,0:T(8,128)} %fusion.30, bf16[64,32,128]{0,1,2:T(8,128)(2,1)S(1)} %copy.24), kind=kLoop, calls=%fused_computation.8 | loop fusion | flops 786432 | bytes 3670016 | tf_op jit(solution)/shard_map/add | solution.py:53
  258.5 2.1 multiply_subtract_fusion
  260.6 3.9 %copy.26 = f32[64,32,128]{2,1,0:T(8,128)} copy(f32[64,32,128]{0,1,2:T(8,128)} %get-tuple-element.21) | data formatting | bytes 2097152
  264.5 2.5 copy.27
  (18 shorter events, 8.9 us)
Async XLA Ops:
  2.5 61.4 %collective-permute-start.1 = (bf16[64,32,128]{2,1,0:T(8,128)(2,1)S(1)}, bf16[64,32,128]{2,1,0:T(8,128)(2,1)}, u32[]{:S(2)}, u32[]{:S(2)}) collective-permute-start(bf16[64,32,128]{2,1,0:T(8,128)(2,1)S(1)} %get-tuple-element.22), channel_id=1, source_target_pairs={{0,1},{1,2},{2,3},{3,4},{4,5},{5,6},{6,7},{7,8},{8,9},{9,10},{10,1... | collective-permute-start | bytes 1572872 | tf_op jit(solution)/shard_map/ppermute | solution.py:10
  5.9 58.0 %collective-permute-start = (bf16[64,32,64]{2,1,0:T(8,128)(2,1)S(1)}, bf16[64,32,64]{2,1,0:T(8,128)(2,1)}, u32[]{:S(2)}, u32[]{:S(2)}) collective-permute-start(bf16[64,32,64]{2,1,0:T(8,128)(2,1)S(1)} %slice.43), channel_id=1, source_target_pairs={{0,2},{1,3},{2,4},{3,5},{4,6},{5,7},{6,8},{7,9},{8,10},{9,11},{10,... | collective-permute-start | bytes 786440 | tf_op jit(solution)/shard_map/ppermute | solution.py:10
  20.6 43.3 %copy-start.2 = (s32[15,128]{1,0:T(8,128)S(1)}, s32[15,128]{1,0:T(8,128)}, u32[]{:S(2)}) copy-start(s32[15,128]{1,0:T(8,128)} %param.9) | copy-start | bytes 23044
  195.6 1.5 copy-start.1
  201.7 49.4 %collective-permute-start.2 = (bf16[64,32,128]{2,1,0:T(8,128)(2,1)}, bf16[64,32,128]{2,1,0:T(8,128)(2,1)}, u32[]{:S(2)}, u32[]{:S(2)}) collective-permute-start(bf16[64,32,128]{2,1,0:T(8,128)(2,1)} %copy.23), channel_id=1, source_target_pairs={{1,0},{2,1},{3,2},{4,3},{5,4},{6,5},{7,6},{8,7},{9,8},{10,9},{11,1... | collective-permute-start | bytes 1572872 | tf_op jit(solution)/shard_map/ppermute | solution.py:10
  209.0 47.7 %collective-permute-start.3 = (bf16[64,32,64]{0,1,2:T(8,128)(2,1)}, bf16[64,32,64]{0,1,2:T(8,128)(2,1)}, u32[]{:S(2)}, u32[]{:S(2)}) collective-permute-start(bf16[64,32,64]{0,1,2:T(8,128)(2,1)} %slice.47), channel_id=1, source_target_pairs={{2,0},{3,1},{4,2},{5,3},{6,4},{7,5},{8,6},{9,7},{10,8},{11,9},{12,... | collective-permute-start | bytes 786440 | tf_op jit(solution)/shard_map/ppermute | solution.py:10
  256.7 1.7 copy-start
where the time goes:
time: 269 us; the launch traced here: 267 us
  local copies, waits for them, and re-layouts  134 us (50%)
  matrix products  72 us (27%)
  blocking collectives  38.7 us (14%)
  other arithmetic  11.4 us (4%)
  starting transfers between devices  10.2 us (4%)
    unnamed x11, local copies, waits for them, and re-layouts  59.5 us
    psum x1, blocking collectives, on_device(): norm = lax.psum(norm_local, 'space')  38.7 us
    dot_general x1, local copies, waits for them, and re-layouts, on_device(): jnp.einsum('nlki,lri->krni', off_tiles, image_rounded, preferred_element_...  27.7 us
    dot_general x1, local copies, waits for them, and re-layouts, on_device(): jnp.einsum('lrt,nit->lrni', table, picker, preferred_element_type=jnp.flo...  27.5 us
    dot_general x1, matrix products, on_device(): jnp.einsum('nlki,lri->krni', off_tiles, image_rounded, preferred_element_...  23.3 us
    dot_general x1, matrix products, on_device(): jnp.einsum('nlki,krni->lri', off_tiles, picked, preferred_element_type=jn...  18.2 us
    dot_general x1, matrix products, on_device(): jnp.einsum('krni,nit->krt', coupled, spreader, precision=highest, preferr...  16.7 us
    ppermute x4, starting transfers between devices, from_behind(): lax.ppermute(value, axis, [(source, source + steps) for source in range(f...  10.2 us
  transfers between devices with their start and end apart: 4, of which 0 were waited for; matrix products, arithmetic and copies ran while one was open for 25% of the time, Pallas kernels for 0%

commit v1 on v0

v1 whole, which is shorter than its diff:
```python
import functools

import jax
import jax.numpy as jnp
from jax import lax
from jax.experimental import pallas as pl
from jax.experimental.pallas import tpu as pltpu
from jax.sharding import PartitionSpec as P

GROUP = 8


def from_behind(value, axis, steps):
    count = lax.axis_size(axis)
    first, last = (max(0, -steps), min(count, count - steps))
    return lax.ppermute(value, axis, [(source, source + steps) for source in range(first, last)])


def turn_kernel(off_ref, diag_ref, out_ref):
    slots, rows, depth, blocks = off_ref.shape
    groups = blocks // GROUP
    for pair in range(rows // 2):
        for m in range((slots + 1) // 2):
            parts = []
            for row in (2 * pair, 2 * pair + 1):
                first = off_ref[2 * m, row]
                second = off_ref[2 * m + 1, row] if 2 * m + 1 < slots else diag_ref[row]
                both = jnp.concatenate([first, second], axis=0).astype(jnp.float32)
                parts.append(both.T.reshape(groups, GROUP, 2 * depth))
            packed = jnp.concatenate(parts, axis=1).astype(jnp.bfloat16)
            out_ref[:, pair * 16 : pair * 16 + 16, m * 2 * depth : (m + 1) * 2 * depth] = packed


def turn_tiles(off_tiles, diag_tiles):
    slots, rows, depth, blocks = off_tiles.shape
    step = 8
    groups = blocks // GROUP
    wide = (slots + 1) * depth
    return pl.pallas_call(
        turn_kernel,
        grid=(rows // step,),
        in_specs=[
            pl.BlockSpec((slots, step, depth, blocks), lambda s: (0, s, 0, 0)),
            pl.BlockSpec((step, depth, blocks), lambda s: (s, 0, 0)),
        ],
        out_specs=pl.BlockSpec((groups, step * GROUP, wide), lambda s: (0, s, 0)),
        out_shape=jax.ShapeDtypeStruct((groups, rows * GROUP, wide), jnp.bfloat16),
        compiler_params=pltpu.CompilerParams(vmem_limit_bytes=40 * 2**20),
        cost_estimate=pl.CostEstimate(flops=0, bytes_accessed=64 * 2**20, transcendentals=0),
        name="turn_tiles",
    )(off_tiles, diag_tiles)


def low_lanes(shape):
    return lax.broadcasted_iota(jnp.int32, shape, len(shape) - 1) < shape[-1] // 2


def main_kernel(
    ids_ref, own_ref, earlier_ref, oldest_ref, t_ref,
    for_oldest_ref, for_earlier_ref, own_out_ref, curve_ref,
    low_table, high_table, low_sum, high_sum, picked, terms,
):
    step = pl.program_id(0)
    half = own_ref.shape[0]
    quarter = oldest_ref.shape[0]
    rhs, lanes = own_ref.shape[1:]
    depth = lanes // 2
    pairs = t_ref.shape[2] // lanes
    starts = (0, 2 * quarter, 2 * quarter + 2 * half)

    @pl.when(step == 0)
    def _():
        low = low_lanes((rhs, lanes))
        for source, start in zip((oldest_ref, earlier_ref, own_ref), starts):
            size = source.shape[0]

            @pl.loop(0, size)
            def _(j):
                page = source[j].astype(jnp.float32)
                other = pltpu.roll(page, depth, 1)
                for table, here in ((low_table, low), (high_table, ~low)):
                    first, second = (page, other) if table is low_table else (other, page)
                    table[start + j] = jnp.where(here, first, 0.0).astype(jnp.bfloat16)
                    table[start + size + j] = jnp.where(here, second, 0.0).astype(jnp.bfloat16)

        @pl.loop(0, low_sum.shape[0])
        def _(j):
            low_sum[j] = jnp.zeros((rhs, lanes), jnp.float32)
            high_sum[j] = jnp.zeros((rhs, lanes), jnp.float32)

        curve_ref[...] = jnp.zeros_like(curve_ref)

    for b in range(GROUP):
        for m in range(pairs):
            first = ids_ref[2 * m, step * GROUP + b]
            second = ids_ref[2 * m + 1, step * GROUP + b]
            picked[b * rhs : (b + 1) * rhs, m * lanes : (m + 1) * lanes] = low_table[first] + high_table[second]

    image = lax.dot_general(
        t_ref[0], picked[...], (((1,), (1,)), ((), ())), preferred_element_type=jnp.float32
    )
    row = lax.broadcasted_iota(jnp.int32, image.shape, 0) % GROUP
    column = lax.broadcasted_iota(jnp.int32, image.shape, 1) // rhs
    image = jnp.where(row == column, image, 0.0)
    rounded = image.astype(jnp.bfloat16)
    curve_ref[...] += jnp.sum(image * rounded.astype(jnp.float32), axis=0, keepdims=True)
    terms[...] = lax.dot_general(
        rounded, t_ref[0], (((0,), (0,)), ((), ())), preferred_element_type=jnp.float32
    )
    for b in range(GROUP):
        for table, odd in ((low_sum, 0), (high_sum, 1)):
            for begin in range(0, pairs, 4):
                ids = [ids_ref[2 * m + odd, step * GROUP + b] for m in range(begin, begin + 4)]
                sums = [
                    table[ids[m - begin]] + terms[b * rhs : (b + 1) * rhs, m * lanes : (m + 1) * lanes]
                    for m in range(begin, begin + 4)
                ]
                for at, value in zip(ids, sums):
                    table[at] = value

    @pl.when(step == pl.num_programs(0) - 1)
    def _():
        low = low_lanes((rhs, lanes))

        def total(t):
            mixed = jnp.where(low, low_sum[t], high_sum[t])
            return mixed + pltpu.roll(mixed, depth, 1)

        for out, start in zip((for_oldest_ref, for_earlier_ref, own_out_ref), starts):
            size = out.shape[0]

            @pl.loop(0, size)
            def _(j):
                out[j] = jnp.where(low, total(start + j), total(start + size + j)).astype(out.dtype)


def main_call(ids, own, earlier, oldest, turned):
    half, rhs, lanes = own.shape
    quarter = oldest.shape[0]
    groups, rows, wide = turned.shape
    pages = 4 * half + 2 * quarter
    whole = lambda shape: pl.BlockSpec(shape, lambda s: (0,) * len(shape))
    return pl.pallas_call(
        main_kernel,
        grid=(groups,),
        in_specs=[
            pl.BlockSpec(memory_space=pltpu.SMEM),
            whole(own.shape),
            whole(earlier.shape),
            whole(oldest.shape),
            pl.BlockSpec((1, rows, wide), lambda s: (s, 0, 0)),
        ],
        out_specs=[whole(oldest.shape), whole(own.shape), whole(own.shape), whole((1, GROUP * rhs))],
        out_shape=[
            jax.ShapeDtypeStruct(oldest.shape, jnp.bfloat16),
            jax.ShapeDtypeStruct(own.shape, jnp.bfloat16),
            jax.ShapeDtypeStruct(own.shape, jnp.float32),
            jax.ShapeDtypeStruct((1, GROUP * rhs), jnp.float32),
        ],
        scratch_shapes=[
            pltpu.VMEM((pages, rhs, lanes), jnp.bfloat16),
            pltpu.VMEM((pages, rhs, lanes), jnp.bfloat16),
            pltpu.VMEM((pages, rhs, lanes), jnp.float32),
            pltpu.VMEM((pages, rhs, lanes), jnp.float32),
            pltpu.VMEM((GROUP * rhs, wide), jnp.bfloat16),
            pltpu.VMEM((GROUP * rhs, wide), jnp.float32),
        ],
        compiler_params=pltpu.CompilerParams(vmem_limit_bytes=48 * 2**20),
        cost_estimate=pl.CostEstimate(flops=8 * 10**9, bytes_accessed=32 * 2**20, transcendentals=0),
        name="image_and_terms",
    )(ids, own, earlier, oldest, turned)


def on_device(right_side, diag_tiles, off_tiles, neighbours):
    depth, rhs, blocks = right_side.shape
    half = blocks // 2
    quarter = half // 2
    device = lax.axis_index("space")
    own = (
        right_side.astype(jnp.bfloat16)
        .reshape(depth, rhs, 2, half)
        .transpose(3, 1, 2, 0)
        .reshape(half, rhs, 2 * depth)
    )
    late = own[:, :, depth:]
    late = jnp.concatenate([late[:quarter], late[quarter:]], axis=2)
    earlier = from_behind(own, "space", 1)
    oldest = from_behind(late, "space", 2)
    turned = turn_tiles(off_tiles, diag_tiles)
    ids = jnp.concatenate(
        [
            neighbours - (device * blocks - blocks - half),
            (blocks + half + jnp.arange(blocks, dtype=jnp.int32))[None],
        ],
        axis=0,
    )
    for_oldest, for_earlier, own_sum, curve_parts = main_call(ids, own, earlier, oldest, turned)
    from_next = from_behind(for_earlier, "space", -1).astype(jnp.float32)
    from_after = from_behind(for_oldest, "space", -2).astype(jnp.float32)
    norm_local = jnp.sum(right_side * right_side, axis=(0, 2))
    curve_local = jnp.sum(curve_parts.reshape(GROUP, rhs), axis=0)
    norm, curve = lax.psum(jnp.stack([norm_local, curve_local]), "space")
    after = jnp.concatenate([from_after[:, :, :depth], from_after[:, :, depth:]], axis=0)
    product = own_sum + from_next + jnp.pad(after, ((0, 0), (0, 0), (depth, 0)))
    product = product.reshape(half, rhs, 2, depth).transpose(3, 1, 2, 0).reshape(depth, rhs, blocks)
    step_size = (norm / curve)[None, :, None]
    solution = step_size * right_side
    residual = right_side - step_size * product
    return (solution, residual)


def solution(mesh):
    placed = (
        P(None, None, ("grp", "space")),
        P(None, None, ("grp", "space")),
        P(None, None, None, ("grp", "space")),
        P(None, ("grp", "space")),
    )
    return jax.shard_map(
        on_device,
        mesh=mesh,
        in_specs=placed,
        out_specs=(P(None, None, ("grp", "space")), P(None, None, ("grp", "space"))),
        check_vma=False,
    )
```

time: 269 us -> 135 us (0.50)
  local copies, waits for them, and re-layouts: 134 us -> 13 us
  matrix products: 72 us -> 0 us
  Pallas kernels: 0 us -> 68 us
  other arithmetic: 11.4 us -> 7.78 us
  blocking collectives: 38.7 us -> 35.9 us
    dot_general x6 -> x0, matrix products: 72 us -> none  [the longest x1 23.3 us: on_device(): jnp.einsum('nlki,lri->krni', off_tiles, image_rounded, preferred_element_...]
    pallas_call x0 -> x2, Pallas kernels: none -> 68 us  [the longest x1 52.9 us: main_call(): pl.pallas_call(main_kernel, grid=(groups,), in_specs=[pl.BlockSpec(memory...]
    dot_general x3 -> x0, local copies, waits for them, and re-layouts: 62.4 us -> none  [the longest x1 27.7 us: on_device(): jnp.einsum('nlki,lri->krni', off_tiles, image_rounded, preferred_element_...]
    unnamed x11 -> x4, local copies, waits for them, and re-layouts: 59.5 us -> 2.01 us
    slice x4 -> x2, local copies, waits for them, and re-layouts: 6.7 us -> 0.37 us  [the longest x1 0.21 us: on_device(): late = jnp.concatenate([late[:quarter], late[quarter:]], axis=2)]
    reshape x0 -> x6, local copies, waits for them, and re-layouts: none -> 6.28 us  [the longest x2 3.75 us: on_device(): product.reshape(half, rhs, 2, depth).transpose(3, 1, 2, 0)]
    transpose x0 -> x1, local copies, waits for them, and re-layouts: none -> 3.83 us  [on_device(): product.reshape(half, rhs, 2, depth).transpose(3, 1, 2, 0)]
    another operation x1, other arithmetic: 3.11 us -> 0.01 us  [on_device(): norm, curve = lax.psum(jnp.stack([norm_local, curve_local]), 'space')]
  transfers between devices with their start and end apart: 4 -> 4, of which waited for: 0 -> 0; matrix products, arithmetic and copies ran while one was open for 25% -> 2% of each run, Pallas kernels for 0% -> 11%
where the time goes in v1:
time: 135 us
  Pallas kernels  68 us (50%)
  blocking collectives  35.9 us (27%)
  local copies, waits for them, and re-layouts  13 us (10%)
  starting transfers between devices  9.39 us (7%)
  other arithmetic  7.78 us (6%)
    pallas_call x1, Pallas kernels, main_call(): pl.pallas_call(main_kernel, grid=(groups,), in_specs=[pl.BlockSpec(memory...  52.9 us
    psum x1, blocking collectives, on_device(): norm, curve = lax.psum(jnp.stack([norm_local, curve_local]), 'space')  35.9 us
    pallas_call x1, Pallas kernels, turn_tiles(): pl.pallas_call(turn_kernel, grid=(rows // step,), in_specs=[pl.BlockSpec(...  15.1 us
    ppermute x4, starting transfers between devices, from_behind(): lax.ppermute(value, axis, [(source, source + steps) for source in range(f...  9.39 us
    transpose x1, local copies, waits for them, and re-layouts, on_device(): product.reshape(half, rhs, 2, depth).transpose(3, 1, 2, 0)  3.83 us
    reshape x2, local copies, waits for them, and re-layouts, on_device(): product.reshape(half, rhs, 2, depth).transpose(3, 1, 2, 0)  3.75 us
    sub x1, other arithmetic, on_device(): residual = right_side - step_size * product  2.87 us
  transfers between devices with their start and end apart: 4, of which 0 were waited for; matrix products, arithmetic and copies ran while one was open for 2% of the time, Pallas kernels for 11%

profile of v1, /device:TPU:0, one launch (start us, length us, event | category | flops | bytes accessed | tf_op | source)
XLA Modules:
  0.0 134.9 jit_solution(17569986320539143983)
XLA Ops:
  0.6 1.9 %multiply_reduce_fusion = (f32[32]{0:T(128)S(1)}, bf16[64,32,128]{2,1,0:T(8,128)(2,1)S(1)}) fusion(f32[64,32,128]{2,1,0:T(8,128)} %param.4), kind=kLoop, calls=%fused_computation.4 | loop fusion | flops 786400 | bytes 1572992 | tf_op jit(solution)/shard_map/reduce_sum | solution.py:200
  2.5 0.4 reshape.36
  3.0 1.6 %copy.6 = bf16[64,32,2,64]{0,2,1,3:T(2,128)(2,1)S(1)} copy(bf16[64,32,2,64]{3,2,1,0:T(2,128)(2,1)S(1)} %reshape.36) | data formatting | bytes 1048576 | tf_op jit(solution)/shard_map/reshape | solution.py:181
  4.5 0.5 reshape.37.own_ref
  5.0 2.4 %collective-permute-start = (bf16[64,32,128]{2,1,0:T(8,128)(2,1)S(1)}, bf16[64,32,128]{2,1,0:T(8,128)(2,1)S(1)}, u32[]{:S(2)}, u32[]{:S(2)}) collective-permute-start(bf16[64,32,128]{2,1,0:T(8,128)(2,1)S(1)} %reshape.37.own_ref), channel_id=1, source_target_pairs={{0,1},{1,2},{2,3},{3,4},{4,5},{5,6},{6,7},{7,8},{8,9},{9,10},{10,1... | collective-permute-start | bytes 1572872 | tf_op jit(solution)/shard_map/ppermute | solution.py:16
  7.4 0.2 fusion.2
  7.6 0.1 pad_maximum_fusion
  7.8 4.4 %collective-permute-start.1 = (bf16[32,32,128]{2,1,0:T(8,128)(2,1)S(1)}, bf16[32,32,128]{2,1,0:T(8,128)(2,1)S(1)}, u32[]{:S(2)}, u32[]{:S(2)}) collective-permute-start(bf16[32,32,128]{2,1,0:T(8,128)(2,1)S(1)} %pad_maximum_fusion), channel_id=1, source_target_pairs={{0,2},{1,3},{2,4},{3,5},{4,6},{5,7},{6,8},{7,9},{8,10},{9,11},{10,... | collective-permute-start | bytes 786440 | tf_op jit(solution)/shard_map/ppermute | solution.py:16
  12.2 0.7 broadcast_subtract_fusion
  12.9 1.2 copy-done
  14.1 15.1 %turn_tiles.1.t_ref = bf16[16,512,1024]{2,1,0:T(8,128)(2,1)} custom-call(bf16[15,64,64,128]{3,2,1,0:T(8,128)(2,1)} %off_ref.1, bf16[64,64,128]{2,1,0:T(8,128)(2,1)S(1)} %copy-done), custom_call_target="tpu_custom_call" | custom-call | bytes 67108864 | tf_op jit(solution)/shard_map/turn_tiles/pallas_call | solution.py:39
  29.3 52.9 %image_and_terms.1 = (bf16[32,32,128]{2,1,0:T(8,128)(2,1)S(1)}, bf16[64,32,128]{2,1,0:T(8,128)(2,1)S(1)}, f32[64,32,128]{2,1,0:T(8,128)S(1)}, f32[1,256]{1,0:T(1,128)S(1)}) custom-call(s32[16,128]{1,0:T(8,128)S(1)} %pad_add_fusion.ids_ref, bf16[64,32,128]{2,1,0:T(8,128)(2,1)S(1)} %reshape.37.own_ref, ...), custom_call_target="tpu_custom_call" | custom-call | flops 8000000000 | bytes 33554432 | tf_op jit(solution)/shard_map/image_and_terms/pallas_call | solution.py:143
  82.2 1.3 collective-permute-start.3
  83.4 1.3 collective-permute-start.2
  84.7 0.5 broadcast.18
  85.3 0.7 reduce.3
  86.0 35.9 %psum.7 = f32[2,32]{1,0:T(2,128)S(1)} all-reduce(f32[2,32]{1,0:T(2,128)S(1)} %pad_maximum_fusion.1), channel_id=1, replica_groups=mesh['grp'=2,'space'=16] {'space'}, use_global_device_ids=true, to_apply=%region_2.0 | all-reduce | flops 64 | bytes 512 | tf_op jit(solution)/shard_map/psum | solution.py:202
  122.0 0.2 fusion.3
  122.2 0.8 copy-done.1
  123.0 1.4 %fusion = f32[64,32,128]{2,1,0:T(8,128)S(1)} fusion(f32[32,32,64]{2,1,0:T(8,128)S(1)} %get-tuple-element.17, f32[32,32,64]{2,1,0:T(8,128)S(1)} %get-tuple-element.16, f32[64,32,128]{2,1,0:T(8,128)S(1)} %get-tuple-element.7, bf16[64,32,128]{2,1,0:T(8,128)(2,1)} %copy-done.1), kind=kLoop, calls=%fused_computation.1 | loop fusion | flops 1835008 | bytes 3145728 | tf_op jit(solution)/shard_map/add | solution.py:204
  124.4 1.2 reshape.39
  125.6 3.8 %copy.7 = f32[64,32,2,64]{3,2,1,0:T(2,128)} copy(f32[64,32,2,64]{0,2,1,3:T(2,128)S(1)} %bitcast.6) | data formatting | bytes 2097152 | tf_op jit(solution)/shard_map/transpose | solution.py:205
  129.4 2.6 %reshape.40 = f32[64,32,128]{2,1,0:T(8,128)S(1)} reshape(f32[64,32,2,64]{3,2,1,0:T(2,128)} %copy.7) | data formatting | bytes 2097152 | tf_op jit(solution)/shard_map/reshape | solution.py:205
  132.0 2.9 %multiply_subtract_fusion = (f32[64,32,128]{2,1,0:T(8,128)}, f32[64,32,128]{2,1,0:T(8,128)}) fusion(f32[64,32,128]{2,1,0:T(8,128)} %param.4, f32[64,32,128]{2,1,0:T(8,128)S(1)} %reshape.40, f32[32]{0:T(128)S(1)} %fusion.1), kind=kLoop, calls=%fused_computation.3 | loop fusion | flops 786432 | bytes 4194432 | tf_op jit(solution)/shard_map/sub | solution.py:208
  (12 shorter events, 0.2 us)
Async XLA Ops:
  5.0 24.3 %collective-permute-start = (bf16[64,32,128]{2,1,0:T(8,128)(2,1)S(1)}, bf16[64,32,128]{2,1,0:T(8,128)(2,1)S(1)}, u32[]{:S(2)}, u32[]{:S(2)}) collective-permute-start(bf16[64,32,128]{2,1,0:T(8,128)(2,1)S(1)} %reshape.37.own_ref), channel_id=1, source_target_pairs={{0,1},{1,2},{2,3},{3,4},{4,5},{5,6},{6,7},{7,8},{8,9},{9,10},{10,1... | collective-permute-start | bytes 1572872 | tf_op jit(solution)/shard_map/ppermute | solution.py:16
  7.8 21.5 %collective-permute-start.1 = (bf16[32,32,128]{2,1,0:T(8,128)(2,1)S(1)}, bf16[32,32,128]{2,1,0:T(8,128)(2,1)S(1)}, u32[]{:S(2)}, u32[]{:S(2)}) collective-permute-start(bf16[32,32,128]{2,1,0:T(8,128)(2,1)S(1)} %pad_maximum_fusion), channel_id=1, source_target_pairs={{0,2},{1,3},{2,4},{3,5},{4,6},{5,7},{6,8},{7,9},{8,10},{9,11},{10,... | collective-permute-start | bytes 786440 | tf_op jit(solution)/shard_map/ppermute | solution.py:16
  12.9 1.2 copy-start
  82.2 39.8 %collective-permute-start.3 = (bf16[32,32,128]{2,1,0:T(8,128)(2,1)S(1)}, bf16[32,32,128]{2,1,0:T(8,128)(2,1)S(1)}, u32[]{:S(2)}, u32[]{:S(2)}) collective-permute-start(bf16[32,32,128]{2,1,0:T(8,128)(2,1)S(1)} %get-tuple-element.9), channel_id=1, source_target_pairs={{2,0},{3,1},{4,2},{5,3},{6,4},{7,5},{8,6},{9,7},{10,8},{11,9},{12,... | collective-permute-start | bytes 786440 | tf_op jit(solution)/shard_map/ppermute | solution.py:16
  83.4 38.7 %collective-permute-start.2 = (bf16[64,32,128]{2,1,0:T(8,128)(2,1)S(1)}, bf16[64,32,128]{2,1,0:T(8,128)(2,1)S(1)}, u32[]{:S(2)}, u32[]{:S(2)}) collective-permute-start(bf16[64,32,128]{2,1,0:T(8,128)(2,1)S(1)} %get-tuple-element.8), channel_id=1, source_target_pairs={{1,0},{2,1},{3,2},{4,3},{5,4},{6,5},{7,6},{8,7},{9,8},{10,9},{11,1... | collective-permute-start | bytes 1572872 | tf_op jit(solution)/shard_map/ppermute | solution.py:16
  122.2 0.8 copy-start.1

commit v2 on v1

--- a/solution.py
+++ b/solution.py
@@ -67,6 +67,11 @@
     depth = lanes // 2
     pairs = t_ref.shape[2] // lanes
     starts = (0, 2 * quarter, 2 * quarter + 2 * half)
+    base = lax.axis_index("space") * (2 * half) - starts[2]
+
+    def page_of(slot, b):
+        block = step * GROUP + b
+        return starts[2] + block if slot == 2 * pairs - 1 else ids_ref[slot, block] - base
 
     @pl.when(step == 0)
     def _():
@@ -74,7 +79,7 @@
         for source, start in zip((oldest_ref, earlier_ref, own_ref), starts):
             size = source.shape[0]
 
-            @pl.loop(0, size)
+            @pl.loop(0, size, unroll=8)
             def _(j):
                 page = source[j].astype(jnp.float32)
                 other = pltpu.roll(page, depth, 1)
@@ -83,7 +88,7 @@
                     table[start + j] = jnp.where(here, first, 0.0).astype(jnp.bfloat16)
                     table[start + size + j] = jnp.where(here, second, 0.0).astype(jnp.bfloat16)
 
-        @pl.loop(0, low_sum.shape[0])
+        @pl.loop(0, low_sum.shape[0], unroll=8)
         def _(j):
             low_sum[j] = jnp.zeros((rhs, lanes), jnp.float32)
             high_sum[j] = jnp.zeros((rhs, lanes), jnp.float32)
@@ -92,25 +97,27 @@
 
     for b in range(GROUP):
         for m in range(pairs):
-            first = ids_ref[2 * m, step * GROUP + b]
-            second = ids_ref[2 * m + 1, step * GROUP + b]
+            first, second = page_of(2 * m, b), page_of(2 * m + 1, b)
             picked[b * rhs : (b + 1) * rhs, m * lanes : (m + 1) * lanes] = low_table[first] + high_table[second]
 
     image = lax.dot_general(
         t_ref[0], picked[...], (((1,), (1,)), ((), ())), preferred_element_type=jnp.float32
     )
-    row = lax.broadcasted_iota(jnp.int32, image.shape, 0) % GROUP
-    column = lax.broadcasted_iota(jnp.int32, image.shape, 1) // rhs
-    image = jnp.where(row == column, image, 0.0)
-    rounded = image.astype(jnp.bfloat16)
-    curve_ref[...] += jnp.sum(image * rounded.astype(jnp.float32), axis=0, keepdims=True)
+    shape = (1, GROUP, image.shape[1])
+    start = lax.broadcasted_iota(jnp.int32, shape, 1) * rhs
+    column = lax.broadcasted_iota(jnp.int32, shape, 2)
+    meant = (column >= start) & (column < start + rhs)
+    image = jnp.where(meant, image.reshape(-1, GROUP, shape[2]), 0.0)
+    rounded = image.reshape(-1, shape[2]).astype(jnp.bfloat16)
+    square = image * rounded.astype(jnp.float32).reshape(image.shape)
+    curve_ref[...] += jnp.sum(square, axis=0)
     terms[...] = lax.dot_general(
         rounded, t_ref[0], (((0,), (0,)), ((), ())), preferred_element_type=jnp.float32
     )
     for b in range(GROUP):
         for table, odd in ((low_sum, 0), (high_sum, 1)):
             for begin in range(0, pairs, 4):
-                ids = [ids_ref[2 * m + odd, step * GROUP + b] for m in range(begin, begin + 4)]
+                ids = [page_of(2 * m + odd, b) for m in range(begin, begin + 4)]
                 sums = [
                     table[ids[m - begin]] + terms[b * rhs : (b + 1) * rhs, m * lanes : (m + 1) * lanes]
                     for m in range(begin, begin + 4)
@@ -129,7 +136,7 @@
         for out, start in zip((for_oldest_ref, for_earlier_ref, own_out_ref), starts):
             size = out.shape[0]
 
-            @pl.loop(0, size)
+            @pl.loop(0, size, unroll=8)
             def _(j):
                 out[j] = jnp.where(low, total(start + j), total(start + size + j)).astype(out.dtype)
 
@@ -150,12 +157,12 @@
             whole(oldest.shape),
             pl.BlockSpec((1, rows, wide), lambda s: (s, 0, 0)),
         ],
-        out_specs=[whole(oldest.shape), whole(own.shape), whole(own.shape), whole((1, GROUP * rhs))],
+        out_specs=[whole(oldest.shape), whole(own.shape), whole(own.shape), whole((GROUP, GROUP * rhs))],
         out_shape=[
             jax.ShapeDtypeStruct(oldest.shape, jnp.bfloat16),
             jax.ShapeDtypeStruct(own.shape, jnp.bfloat16),
             jax.ShapeDtypeStruct(own.shape, jnp.float32),
-            jax.ShapeDtypeStruct((1, GROUP * rhs), jnp.float32),
+            jax.ShapeDtypeStruct((GROUP, GROUP * rhs), jnp.float32),
         ],
         scratch_shapes=[
             pltpu.VMEM((pages, rhs, lanes), jnp.bfloat16),
@@ -171,42 +178,180 @@
     )(ids, own, earlier, oldest, turned)
 
 
-def on_device(right_side, diag_tiles, off_tiles, neighbours):
+def prepare_kernel(x_ref, own_ref, late_ref, wide):
+    half, rhs, lanes = own_ref.shape
+    quarter = late_ref.shape[0]
+    depth = lanes // 2
+    for r in range(rhs):
+        turned = x_ref[:, r, :].T
+        wide[:, r, :] = jnp.concatenate([turned[:half], turned[half:]], axis=1)
+    own_ref[...] = wide[...].astype(jnp.bfloat16)
+    low = low_lanes((quarter, rhs, lanes))
+    first = pltpu.roll(wide[:quarter], depth, 2)
+    late_ref[...] = jnp.where(low, first, wide[quarter:]).astype(jnp.bfloat16)
+
+
+def prepare(right_side):
     depth, rhs, blocks = right_side.shape
     half = blocks // 2
-    quarter = half // 2
-    device = lax.axis_index("space")
-    own = (
-        right_side.astype(jnp.bfloat16)
-        .reshape(depth, rhs, 2, half)
-        .transpose(3, 1, 2, 0)
-        .reshape(half, rhs, 2 * depth)
-    )
-    late = own[:, :, depth:]
-    late = jnp.concatenate([late[:quarter], late[quarter:]], axis=2)
+    return pl.pallas_call(
+        prepare_kernel,
+        out_shape=[
+            jax.ShapeDtypeStruct((half, rhs, 2 * depth), jnp.bfloat16),
+            jax.ShapeDtypeStruct((half // 2, rhs, 2 * depth), jnp.bfloat16),
+        ],
+        scratch_shapes=[pltpu.VMEM((half, rhs, 2 * depth), jnp.float32)],
+        compiler_params=pltpu.CompilerParams(vmem_limit_bytes=24 * 2**20),
+        name="prepare",
+    )(right_side)
+
+
+def finish_kernel(
+    count, oldest_ref, earlier_ref, own_ref, curve_ref, x_ref, solution_ref, residual_ref,
+    after, following, parts, part, turned, small_sent, small_got, sent, got,
+):
+    mesh_ids = pl.DeviceIdType.MESH
+    me = lax.axis_index("space")
+    depth, rhs, blocks = x_ref.shape
+    half, _, lanes = own_ref.shape
+    quarter = oldest_ref.shape[0]
+    row = lax.broadcasted_iota(jnp.int32, (rhs, lanes), 0)
+    lane = lax.broadcasted_iota(jnp.int32, (rhs, lanes), 1)
+    diagonal = row == lane
+
+    barrier = pltpu.get_barrier_semaphore()
+
+    @pl.loop(1, count)
+    def _(k):
+        pl.semaphore_signal(
+            barrier, inc=1, device_id={"space": lax.rem(me + k, count)}, device_id_type=mesh_ids
+        )
+
+    squares = jnp.zeros((rhs, blocks), jnp.float32)
+    for k in range(depth):
+        squares = squares + x_ref[k] * x_ref[k]
+    norms = jnp.sum(squares, axis=1, keepdims=True)
+    part[...] = jnp.zeros_like(part)
+    part[0:1, :] = jnp.sum(jnp.where(diagonal, norms, 0.0), axis=0, keepdims=True)
+    curves = jnp.sum(curve_ref[...], axis=0, keepdims=True)
+    curves = curves[:, :lanes] + curves[:, lanes:]
+    folded = curves
+    for turn in range(rhs, lanes, rhs):
+        folded = folded + pltpu.roll(curves, turn, 1)
+    part[1:2, :] = folded
+
+    pl.semaphore_wait(barrier, count - 1)
+
+    def small(k, slot):
+        return pltpu.make_async_remote_copy(
+            src_ref=part,
+            dst_ref=parts.at[slot],
+            send_sem=small_sent.at[k],
+            recv_sem=small_got.at[slot],
+            device_id={"space": lax.rem(me + k, count)},
+            device_id_type=mesh_ids,
+        )
+
+    @pl.loop(1, count)
+    def _(k):
+        small(k, me).start()
+
+    def behind(source, landing, steps):
+        return pltpu.make_async_remote_copy(
+            src_ref=source,
+            dst_ref=landing,
+            send_sem=sent.at[steps - 1],
+            recv_sem=got.at[steps - 1],
+            device_id={"space": lax.rem(me + count - steps, count)},
+            device_id_type=mesh_ids,
+        )
+
+    moves = (behind(earlier_ref, following, 1), behind(oldest_ref, after, 2))
+    for steps, move in enumerate(moves, 1):
+
+        @pl.when(me >= steps)
+        def _():
+            move.start()
+
+    parts[me] = part[...]
+
+    @pl.loop(1, count)
+    def _(k):
+        small(k, lax.rem(me + k, count)).wait_recv()
+
+    total = parts[0]
+    for slot in range(1, count):
+        total = total + parts[slot]
+    ratio = total[0:1, :] / total[1:2, :]
+    scale = jnp.sum(jnp.where(diagonal, ratio, 0.0), axis=1, keepdims=True)
+    for k in range(depth):
+        solution_ref[k] = scale * x_ref[k]
+
+    for steps, (move, landing) in enumerate(zip(moves, (following, after)), 1):
+
+        @pl.when(me < count - steps)
+        def _():
+            move.wait_recv()
+
+        @pl.when(me >= count - steps)
+        def _():
+            landing[...] = jnp.zeros_like(landing)
+
+    low = low_lanes((rhs, lanes))
+    for j in range(quarter):
+        page = after[j].astype(jnp.float32)
+        own_ref_low = jnp.where(low, 0.0, pltpu.roll(page, depth, 1))
+        turned[j] = own_ref[j] + following[j].astype(jnp.float32) + own_ref_low
+        at = quarter + j
+        turned[at] = own_ref[at] + following[at].astype(jnp.float32) + jnp.where(low, 0.0, page)
+    for r in range(rhs):
+        side = turned[:, r, :].T
+        side = jnp.concatenate([side[:depth], side[depth:]], axis=1)
+        residual_ref[:, r, :] = x_ref[:, r, :] - scale[r : r + 1] * side
+
+    @pl.loop(1, count)
+    def _(k):
+        small(k, me).wait_send()
+
+    for steps, move in enumerate(moves, 1):
+
+        @pl.when(me >= steps)
+        def _():
+            move.wait_send()
+
+
+def finish(count, for_oldest, for_earlier, own_sum, curve_parts, right_side):
+    vmem = pl.BlockSpec(memory_space=pltpu.VMEM)
+    return pl.pallas_call(
+        functools.partial(finish_kernel, count),
+        in_specs=[vmem] * 5,
+        out_specs=[vmem] * 2,
+        out_shape=[jax.ShapeDtypeStruct(right_side.shape, jnp.float32)] * 2,
+        scratch_shapes=[
+            pltpu.VMEM(for_oldest.shape, jnp.bfloat16),
+            pltpu.VMEM(for_earlier.shape, jnp.bfloat16),
+            pltpu.VMEM((count, 8, own_sum.shape[2]), jnp.float32),
+            pltpu.VMEM((8, own_sum.shape[2]), jnp.float32),
+            pltpu.VMEM(own_sum.shape, jnp.float32),
+            pltpu.SemaphoreType.DMA((count,)),
+            pltpu.SemaphoreType.DMA((count,)),
+            pltpu.SemaphoreType.DMA((2,)),
+            pltpu.SemaphoreType.DMA((2,)),
+        ],
+        compiler_params=pltpu.CompilerParams(
+            collective_id=0, has_side_effects=True, vmem_limit_bytes=24 * 2**20
+        ),
+        name="finish",
+    )(for_oldest, for_earlier, own_sum, curve_parts, right_side)
+
+
+def on_device(count, right_side, diag_tiles, off_tiles, neighbours):
+    own, late = prepare(right_side)
     earlier = from_behind(own, "space", 1)
     oldest = from_behind(late, "space", 2)
     turned = turn_tiles(off_tiles, diag_tiles)
-    ids = jnp.concatenate(
-        [
-            neighbours - (device * blocks - blocks - half),
-            (blocks + half + jnp.arange(blocks, dtype=jnp.int32))[None],
-        ],
-        axis=0,
-    )
-    for_oldest, for_earlier, own_sum, curve_parts = main_call(ids, own, earlier, oldest, turned)
-    from_next = from_behind(for_earlier, "space", -1).astype(jnp.float32)
-    from_after = from_behind(for_oldest, "space", -2).astype(jnp.float32)
-    norm_local = jnp.sum(right_side * right_side, axis=(0, 2))
-    curve_local = jnp.sum(curve_parts.reshape(GROUP, rhs), axis=0)
-    norm, curve = lax.psum(jnp.stack([norm_local, curve_local]), "space")
-    after = jnp.concatenate([from_after[:, :, :depth], from_after[:, :, depth:]], axis=0)
-    product = own_sum + from_next + jnp.pad(after, ((0, 0), (0, 0), (depth, 0)))
-    product = product.reshape(half, rhs, 2, depth).transpose(3, 1, 2, 0).reshape(depth, rhs, blocks)
-    step_size = (norm / curve)[None, :, None]
-    solution = step_size * right_side
-    residual = right_side - step_size * product
-    return (solution, residual)
+    for_oldest, for_earlier, own_sum, curve_parts = main_call(neighbours, own, earlier, oldest, turned)
+    return tuple(finish(count, for_oldest, for_earlier, own_sum, curve_parts, right_side))
 
 
 def solution(mesh):
@@ -217,7 +362,7 @@
         P(None, ("grp", "space")),
     )
     return jax.shard_map(
-        on_device,
+        functools.partial(on_device, mesh.shape["space"]),
         mesh=mesh,
         in_specs=placed,
         out_specs=(P(None, None, ("grp", "space")), P(None, None, ("grp", "space"))),

time: 135 us -> 81.5 us (0.60)
  blocking collectives: 35.9 us -> 0 us
  local copies, waits for them, and re-layouts: 13 us -> 4.39 us
  other arithmetic: 7.78 us -> 0 us
  starting transfers between devices: 9.39 us -> 6.81 us
    psum x1 -> x0, blocking collectives: 35.9 us -> none  [on_device(): norm, curve = lax.psum(jnp.stack([norm_local, curve_local]), 'space')]
    pallas_call x0 -> x2, Pallas kernels: none -> 22.2 us  [the longest x1 20.5 us: finish(): pl.pallas_call(functools.partial(finish_kernel, count), in_specs=[vmem] *...]
    pallas_call x1, Pallas kernels: 52.9 us -> 31.9 us  [main_call(): pl.pallas_call(main_kernel, grid=(groups,), in_specs=[pl.BlockSpec(memory...]
    reshape x6 -> x0, local copies, waits for them, and re-layouts: 6.28 us -> none  [the longest x2 3.75 us: on_device(): product.reshape(half, rhs, 2, depth).transpose(3, 1, 2, 0)]
    transpose x1 -> x0, local copies, waits for them, and re-layouts: 3.83 us -> none  [on_device(): product.reshape(half, rhs, 2, depth).transpose(3, 1, 2, 0)]
    sub x2 -> x0, other arithmetic: 3.57 us -> none  [the longest x1 2.87 us: on_device(): residual = right_side - step_size * product]
    ppermute x4 -> x2, starting transfers between devices: 9.39 us -> 6.81 us  [from_behind(): lax.ppermute(value, axis, [(source, source + steps) for source in range(f...]
    unnamed x4 -> x10, local copies, waits for them, and re-layouts: 2.01 us -> 4.39 us
  transfers between devices with their start and end apart: 4 -> 2, of which waited for: 0 -> 0; matrix products, arithmetic and copies ran while one was open for 2% -> 0% of each run, Pallas kernels for 11% -> 19%
where the time goes in v2:
time: 81.5 us; the launch traced here: 81.1 us
  Pallas kernels  69.2 us (85%)
  starting transfers between devices  6.81 us (8%)
  local copies, waits for them, and re-layouts  4.39 us (5%)
    pallas_call x1, Pallas kernels, main_call(): pl.pallas_call(main_kernel, grid=(groups,), in_specs=[pl.BlockSpec(memory...  31.9 us
    pallas_call x1, Pallas kernels, finish(): pl.pallas_call(functools.partial(finish_kernel, count), in_specs=[vmem] *...  20.5 us
    pallas_call x1, Pallas kernels, turn_tiles(): pl.pallas_call(turn_kernel, grid=(rows // step,), in_specs=[pl.BlockSpec(...  15.1 us
    ppermute x2, starting transfers between devices, from_behind(): lax.ppermute(value, axis, [(source, source + steps) for source in range(f...  6.81 us
    unnamed x10, local copies, waits for them, and re-layouts  4.39 us
    pallas_call x1, Pallas kernels, prepare(): pl.pallas_call(prepare_kernel, out_shape=[jax.ShapeDtypeStruct((half, rhs...  1.66 us
  transfers between devices with their start and end apart: 2, of which 0 were waited for; matrix products, arithmetic and copies ran while one was open for 0% of the time, Pallas kernels for 19%

profile of v2, /device:TPU:0, one launch (start us, length us, event | category | flops | bytes accessed | tf_op | source)
XLA Modules:
  0.0 81.1 jit_solution(5437903852397549987)
XLA Ops:
  0.6 0.0 copy-start
  0.6 1.2 %copy-done = f32[64,32,128]{2,1,0:T(8,128)S(1)} copy-done((f32[64,32,128]{2,1,0:T(8,128)S(1)}, f32[64,32,128]{2,1,0:T(8,128)}, u32[]{:S(2)}) %copy-start) | copy-done | bytes 1048600
  1.9 1.7 %prepare.1 = (bf16[64,32,128]{2,1,0:T(8,128)(2,1)S(1)}, bf16[32,32,128]{2,1,0:T(8,128)(2,1)S(1)}) custom-call(f32[64,32,128]{2,1,0:T(8,128)S(1)} %copy-done), custom_call_target="tpu_custom_call" | custom-call | tf_op jit(solution)/shard_map/prepare/pallas_call | solution.py:197
  3.5 2.4 %collective-permute-start = (bf16[64,32,128]{2,1,0:T(8,128)(2,1)S(1)}, bf16[64,32,128]{2,1,0:T(8,128)(2,1)S(1)}, u32[]{:S(2)}, u32[]{:S(2)}) collective-permute-start(bf16[64,32,128]{2,1,0:T(8,128)(2,1)S(1)} %get-tuple-element.8.own_ref), channel_id=1, source_target_pairs={{0,1},{1,2},{2,3},{3,4},{4,5},{5,6},{6,7},{7,8},{8,9},{9,10},{10,1... | collective-permute-start | bytes 1572872 | tf_op jit(solution)/shard_map/ppermute | solution.py:16
  5.9 4.4 %collective-permute-start.1 = (bf16[32,32,128]{2,1,0:T(8,128)(2,1)S(1)}, bf16[32,32,128]{2,1,0:T(8,128)(2,1)S(1)}, u32[]{:S(2)}, u32[]{:S(2)}) collective-permute-start(bf16[32,32,128]{2,1,0:T(8,128)(2,1)S(1)} %get-tuple-element.9), channel_id=1, source_target_pairs={{0,2},{1,3},{2,4},{3,5},{4,6},{5,7},{6,8},{7,9},{8,10},{9,11},{10,... | collective-permute-start | bytes 786440 | tf_op jit(solution)/shard_map/ppermute | solution.py:16
  10.3 0.0 copy-start.2
  10.4 1.2 %copy-done.2 = bf16[64,64,128]{2,1,0:T(8,128)(2,1)S(1)} copy-done((bf16[64,64,128]{2,1,0:T(8,128)(2,1)S(1)}, bf16[64,64,128]{2,1,0:T(8,128)(2,1)}, u32[]{:S(2)}) %copy-start.2) | copy-done | bytes 1048600
  11.6 0.0 copy-start.3
  11.6 15.1 %turn_tiles.1.t_ref = bf16[16,512,1024]{2,1,0:T(8,128)(2,1)} custom-call(bf16[15,64,64,128]{3,2,1,0:T(8,128)(2,1)} %off_ref.1, bf16[64,64,128]{2,1,0:T(8,128)(2,1)S(1)} %copy-done.2), custom_call_target="tpu_custom_call" | custom-call | bytes 67108864 | tf_op jit(solution)/shard_map/turn_tiles/pallas_call | solution.py:39
  26.7 0.0 copy-start.1
  26.7 0.0 collective-permute-done.1.oldest_ref
  26.7 0.0 collective-permute-done.earlier_ref
  26.7 0.0 copy-done.3
  26.7 31.9 %image_and_terms.1 = (bf16[32,32,128]{2,1,0:T(8,128)(2,1)S(1)}, bf16[64,32,128]{2,1,0:T(8,128)(2,1)S(1)}, f32[64,32,128]{2,1,0:T(8,128)S(1)}, f32[8,256]{1,0:T(8,128)S(1)}) custom-call(s32[15,128]{1,0:T(8,128)S(1)} %copy-done.3, bf16[64,32,128]{2,1,0:T(8,128)(2,1)S(1)} %get-tuple-element.8.own_ref, ...), custom_call_target="tpu_custom_call" | custom-call | flops 8000000000 | bytes 33554432 | tf_op jit(solution)/shard_map/image_and_terms/pallas_call | solution.py:150
  58.6 0.0 copy-done.1
  58.6 20.5 %finish.1 = (f32[64,32,128]{2,1,0:T(8,128)S(1)}, f32[64,32,128]{2,1,0:T(8,128)S(1)}) custom-call(bf16[32,32,128]{2,1,0:T(8,128)(2,1)S(1)} %get-tuple-element.10.oldest_ref, bf16[64,32,128]{2,1,0:T(8,128)(2,1)S(1)} %get-tuple-element.11.earlier_ref, f32[64,32,128]{2,1,0:T(8,128)S(1)} %get-tuple-element.12.own_ref, f32[8,256]{1,0:T(8,128)S(1)} %get-tuple-element.13.curve_ref, ...), custom_call_target="tpu_custom_call" | custom-call | tf_op jit(solution)/shard_map/finish/pallas_call | solution.py:325
  79.2 1.0 %copy.8 = f32[64,32,128]{2,1,0:T(8,128)} copy(f32[64,32,128]{2,1,0:T(8,128)S(1)} %get-tuple-element.16) | data formatting | bytes 2097152
  80.1 1.0 %copy.9 = f32[64,32,128]{2,1,0:T(8,128)} copy(f32[64,32,128]{2,1,0:T(8,128)S(1)} %get-tuple-element.17) | data formatting | bytes 2097152
Async XLA Ops:
  0.6 1.2 %copy-start = (f32[64,32,128]{2,1,0:T(8,128)S(1)}, f32[64,32,128]{2,1,0:T(8,128)}, u32[]{:S(2)}) copy-start(f32[64,32,128]{2,1,0:T(8,128)} %x_ref.3) | copy-start | bytes 3145732
  3.5 23.2 %collective-permute-start = (bf16[64,32,128]{2,1,0:T(8,128)(2,1)S(1)}, bf16[64,32,128]{2,1,0:T(8,128)(2,1)S(1)}, u32[]{:S(2)}, u32[]{:S(2)}) collective-permute-start(bf16[64,32,128]{2,1,0:T(8,128)(2,1)S(1)} %get-tuple-element.8.own_ref), channel_id=1, source_target_pairs={{0,1},{1,2},{2,3},{3,4},{4,5},{5,6},{6,7},{7,8},{8,9},{9,10},{10,1... | collective-permute-start | bytes 1572872 | tf_op jit(solution)/shard_map/ppermute | solution.py:16
  5.9 20.8 %collective-permute-start.1 = (bf16[32,32,128]{2,1,0:T(8,128)(2,1)S(1)}, bf16[32,32,128]{2,1,0:T(8,128)(2,1)S(1)}, u32[]{:S(2)}, u32[]{:S(2)}) collective-permute-start(bf16[32,32,128]{2,1,0:T(8,128)(2,1)S(1)} %get-tuple-element.9), channel_id=1, source_target_pairs={{0,2},{1,3},{2,4},{3,5},{4,6},{5,7},{6,8},{7,9},{8,10},{9,11},{10,... | collective-permute-start | bytes 786440 | tf_op jit(solution)/shard_map/ppermute | solution.py:16
  10.3 1.2 %copy-start.2 = (bf16[64,64,128]{2,1,0:T(8,128)(2,1)S(1)}, bf16[64,64,128]{2,1,0:T(8,128)(2,1)}, u32[]{:S(2)}) copy-start(bf16[64,64,128]{2,1,0:T(8,128)(2,1)} %diag_ref.1) | copy-start | bytes 3145732
  11.6 15.1 %copy-start.3 = (s32[15,128]{1,0:T(8,128)S(1)}, s32[15,128]{1,0:T(8,128)}, u32[]{:S(2)}) copy-start(s32[15,128]{1,0:T(8,128)} %ids_ref.1) | copy-start | bytes 23044
  26.7 31.9 %copy-start.1 = (f32[64,32,128]{2,1,0:T(8,128)S(1)}, f32[64,32,128]{2,1,0:T(8,128)}, u32[]{:S(2)}) copy-start(f32[64,32,128]{2,1,0:T(8,128)} %x_ref.3) | copy-start | bytes 3145732

commit v3 on v2

--- a/solution.py
+++ b/solution.py
@@ -8,51 +8,146 @@
 from jax.sharding import PartitionSpec as P
 
 GROUP = 8
-
-
-def from_behind(value, axis, steps):
-    count = lax.axis_size(axis)
-    first, last = (max(0, -steps), min(count, count - steps))
-    return lax.ppermute(value, axis, [(source, source + steps) for source in range(first, last)])
-
-
-def turn_kernel(off_ref, diag_ref, out_ref):
-    slots, rows, depth, blocks = off_ref.shape
+TOGETHER = 2
+TURN_MIB = 40
+MAIN_MIB = 40
+
+
+def low_lanes(shape):
+    return lax.broadcasted_iota(jnp.int32, shape, len(shape) - 1) < shape[-1] // 2
+
+
+def turn_kernel(
+    count, x_ref, off_ref, diag_ref, own_ref, earlier_ref, oldest_ref, out_ref,
+    wide, own, late, following, after, sent, got,
+):
+    mesh_ids = pl.DeviceIdType.MESH
+    me = lax.axis_index("space")
+    at = pl.program_id(0)
+    slots, step, depth, blocks = off_ref.shape
     groups = blocks // GROUP
-    for pair in range(rows // 2):
+    half, rhs, _ = own.shape
+    quarter = late.shape[0]
+
+    def ahead(source, landing, hops):
+        return pltpu.make_async_remote_copy(
+            src_ref=source,
+            dst_ref=landing,
+            send_sem=sent.at[hops - 1],
+            recv_sem=got.at[hops - 1],
+            device_id={"space": lax.rem(me + hops, count)},
+            device_id_type=mesh_ids,
+        )
+
+    moves = (ahead(own, following, 1), ahead(late, after, 2))
+
+    @pl.when(at == 0)
+    def _():
+        barrier = pltpu.get_barrier_semaphore()
+        for hops in (1, 2):
+
+            @pl.when(me >= hops)
+            def _():
+                pl.semaphore_signal(
+                    barrier, inc=1, device_id={"space": me - hops}, device_id_type=mesh_ids
+                )
+
+        for r in range(rhs):
+            turned = x_ref[:, r, :].T
+            wide[:, r, :] = jnp.concatenate([turned[:half], turned[half:]], axis=1)
+        own[...] = wide[...].astype(jnp.bfloat16)
+        low = low_lanes((quarter, rhs, 2 * depth))
+        first = pltpu.roll(wide[:quarter], depth, 2)
+        late[...] = jnp.where(low, first, wide[quarter:]).astype(jnp.bfloat16)
+
+        @pl.when(me < count - 2)
+        def _():
+            pl.semaphore_wait(barrier, 2)
+
+        @pl.when(me == count - 2)
+        def _():
+            pl.semaphore_wait(barrier, 1)
+
+        for hops, move in enumerate(moves, 1):
+
+            @pl.when(me < count - hops)
+            def _():
+                move.start()
+
+    for pair in range(step // 2):
         for m in range((slots + 1) // 2):
             parts = []
             for row in (2 * pair, 2 * pair + 1):
                 first = off_ref[2 * m, row]
-                second = off_ref[2 * m + 1, row] if 2 * m + 1 < slots else diag_ref[row]
+                last = 2 * m + 1 == slots
+                second = diag_ref[row] if last else off_ref[2 * m + 1, row]
                 both = jnp.concatenate([first, second], axis=0).astype(jnp.float32)
                 parts.append(both.T.reshape(groups, GROUP, 2 * depth))
             packed = jnp.concatenate(parts, axis=1).astype(jnp.bfloat16)
             out_ref[:, pair * 16 : pair * 16 + 16, m * 2 * depth : (m + 1) * 2 * depth] = packed
 
-
-def turn_tiles(off_tiles, diag_tiles):
+    @pl.when(at == pl.num_programs(0) - 1)
+    def _():
+        own_ref[...] = own[...]
+        for hops, (move, landing, out) in enumerate(
+            zip(moves, (following, after), (earlier_ref, oldest_ref)), 1
+        ):
+
+            @pl.when(me >= hops)
+            def _():
+                move.wait_recv()
+                out[...] = landing[...]
+
+            @pl.when(me < hops)
+            def _():
+                out[...] = jnp.zeros_like(out)
+
+            @pl.when(me < count - hops)
+            def _():
+                move.wait_send()
+
+
+def turn_tiles(count, right_side, off_tiles, diag_tiles):
     slots, rows, depth, blocks = off_tiles.shape
+    rhs = right_side.shape[1]
     step = 8
     groups = blocks // GROUP
+    half = blocks // 2
     wide = (slots + 1) * depth
+    own = jax.ShapeDtypeStruct((half, rhs, 2 * depth), jnp.bfloat16)
+    late = jax.ShapeDtypeStruct((half // 2, rhs, 2 * depth), jnp.bfloat16)
+    whole = lambda shape: pl.BlockSpec(shape, lambda s: (0,) * len(shape))
     return pl.pallas_call(
-        turn_kernel,
+        functools.partial(turn_kernel, count),
         grid=(rows // step,),
         in_specs=[
+            whole(right_side.shape),
             pl.BlockSpec((slots, step, depth, blocks), lambda s: (0, s, 0, 0)),
             pl.BlockSpec((step, depth, blocks), lambda s: (s, 0, 0)),
         ],
-        out_specs=pl.BlockSpec((groups, step * GROUP, wide), lambda s: (0, s, 0)),
-        out_shape=jax.ShapeDtypeStruct((groups, rows * GROUP, wide), jnp.bfloat16),
-        compiler_params=pltpu.CompilerParams(vmem_limit_bytes=40 * 2**20),
-        cost_estimate=pl.CostEstimate(flops=0, bytes_accessed=64 * 2**20, transcendentals=0),
+        out_specs=[
+            whole(own.shape),
+            whole(own.shape),
+            whole(late.shape),
+            pl.BlockSpec((groups, step * GROUP, wide), lambda s: (0, s, 0)),
+        ],
+        out_shape=[
+            own, own, late, jax.ShapeDtypeStruct((groups, rows * GROUP, wide), jnp.bfloat16)
+        ],
+        scratch_shapes=[
+            pltpu.VMEM(own.shape, jnp.float32),
+            pltpu.VMEM(own.shape, jnp.bfloat16),
+            pltpu.VMEM(late.shape, jnp.bfloat16),
+            pltpu.VMEM(own.shape, jnp.bfloat16),
+            pltpu.VMEM(late.shape, jnp.bfloat16),
+            pltpu.SemaphoreType.DMA((2,)),
+            pltpu.SemaphoreType.DMA((2,)),
+        ],
+        compiler_params=pltpu.CompilerParams(
+            collective_id=1, has_side_effects=True, vmem_limit_bytes=TURN_MIB * 2**20
+        ),
         name="turn_tiles",
-    )(off_tiles, diag_tiles)
-
-
-def low_lanes(shape):
-    return lax.broadcasted_iota(jnp.int32, shape, len(shape) - 1) < shape[-1] // 2
+    )(right_side, off_tiles, diag_tiles)
 
 
 def main_kernel(
@@ -70,7 +165,7 @@
     base = lax.axis_index("space") * (2 * half) - starts[2]
 
     def page_of(slot, b):
-        block = step * GROUP + b
+        block = step * (TOGETHER * GROUP) + b
         return starts[2] + block if slot == 2 * pairs - 1 else ids_ref[slot, block] - base
 
     @pl.when(step == 0)
@@ -95,35 +190,47 @@
 
         curve_ref[...] = jnp.zeros_like(curve_ref)
 
-    for b in range(GROUP):
-        for m in range(pairs):
-            first, second = page_of(2 * m, b), page_of(2 * m + 1, b)
-            picked[b * rhs : (b + 1) * rhs, m * lanes : (m + 1) * lanes] = low_table[first] + high_table[second]
-
-    image = lax.dot_general(
-        t_ref[0], picked[...], (((1,), (1,)), ((), ())), preferred_element_type=jnp.float32
-    )
-    shape = (1, GROUP, image.shape[1])
-    start = lax.broadcasted_iota(jnp.int32, shape, 1) * rhs
-    column = lax.broadcasted_iota(jnp.int32, shape, 2)
-    meant = (column >= start) & (column < start + rhs)
-    image = jnp.where(meant, image.reshape(-1, GROUP, shape[2]), 0.0)
-    rounded = image.reshape(-1, shape[2]).astype(jnp.bfloat16)
-    square = image * rounded.astype(jnp.float32).reshape(image.shape)
-    curve_ref[...] += jnp.sum(square, axis=0)
-    terms[...] = lax.dot_general(
-        rounded, t_ref[0], (((0,), (0,)), ((), ())), preferred_element_type=jnp.float32
-    )
-    for b in range(GROUP):
-        for table, odd in ((low_sum, 0), (high_sum, 1)):
-            for begin in range(0, pairs, 4):
-                ids = [page_of(2 * m + odd, b) for m in range(begin, begin + 4)]
-                sums = [
-                    table[ids[m - begin]] + terms[b * rhs : (b + 1) * rhs, m * lanes : (m + 1) * lanes]
-                    for m in range(begin, begin + 4)
-                ]
-                for at, value in zip(ids, sums):
-                    table[at] = value
+    rows = t_ref.shape[1]
+    column = lax.broadcasted_iota(jnp.int32, (1, rows), 1) & (GROUP - 1)
+
+    for g in range(TOGETHER):
+        for b in range(GROUP):
+            for m in range(pairs):
+                first, second = page_of(2 * m, g * GROUP + b), page_of(2 * m + 1, g * GROUP + b)
+                picked[g, b * rhs : (b + 1) * rhs, m * lanes : (m + 1) * lanes] = (
+                    low_table[first] + high_table[second]
+                )
+    for g in range(TOGETHER):
+        image = lax.dot_general(
+            picked[g], t_ref[g], (((1,), (1,)), ((), ())), preferred_element_type=jnp.float32
+        )
+        image = jnp.concatenate(
+            [jnp.where(column == c, image[c * rhs : (c + 1) * rhs], 0.0) for c in range(GROUP)],
+            axis=0,
+        )
+        rounded = image.astype(jnp.bfloat16)
+        square = image * rounded.astype(jnp.float32)
+        curve = curve_ref[...]
+        for c in range(GROUP):
+            for lane in range(0, rows, lanes):
+                curve = curve + square[c * rhs : (c + 1) * rhs, lane : lane + lanes]
+        curve_ref[...] = curve
+        terms[g] = lax.dot_general(
+            rounded, t_ref[g], (((1,), (0,)), ((), ())), preferred_element_type=jnp.float32
+        )
+    for g in range(TOGETHER):
+        for b in range(GROUP):
+            for table, odd in ((low_sum, 0), (high_sum, 1)):
+                for begin in range(0, pairs, 4):
+                    span = range(begin, begin + 4)
+                    ids = [page_of(2 * m + odd, g * GROUP + b) for m in span]
+                    sums = [
+                        table[at]
+                        + terms[g, b * rhs : (b + 1) * rhs, m * lanes : (m + 1) * lanes]
+                        for at, m in zip(ids, span)
+                    ]
+                    for at, value in zip(ids, sums):
+                        table[at] = value
 
     @pl.when(step == pl.num_programs(0) - 1)
     def _():
@@ -149,61 +256,33 @@
     whole = lambda shape: pl.BlockSpec(shape, lambda s: (0,) * len(shape))
     return pl.pallas_call(
         main_kernel,
-        grid=(groups,),
+        grid=(groups // TOGETHER,),
         in_specs=[
             pl.BlockSpec(memory_space=pltpu.SMEM),
             whole(own.shape),
             whole(earlier.shape),
             whole(oldest.shape),
-            pl.BlockSpec((1, rows, wide), lambda s: (s, 0, 0)),
-        ],
-        out_specs=[whole(oldest.shape), whole(own.shape), whole(own.shape), whole((GROUP, GROUP * rhs))],
+            pl.BlockSpec((TOGETHER, rows, wide), lambda s: (s, 0, 0)),
+        ],
+        out_specs=[whole(oldest.shape), whole(own.shape), whole(own.shape), whole((rhs, lanes))],
         out_shape=[
             jax.ShapeDtypeStruct(oldest.shape, jnp.bfloat16),
             jax.ShapeDtypeStruct(own.shape, jnp.bfloat16),
             jax.ShapeDtypeStruct(own.shape, jnp.float32),
-            jax.ShapeDtypeStruct((GROUP, GROUP * rhs), jnp.float32),
+            jax.ShapeDtypeStruct((rhs, lanes), jnp.float32),
         ],
         scratch_shapes=[
             pltpu.VMEM((pages, rhs, lanes), jnp.bfloat16),
             pltpu.VMEM((pages, rhs, lanes), jnp.bfloat16),
             pltpu.VMEM((pages, rhs, lanes), jnp.float32),
             pltpu.VMEM((pages, rhs, lanes), jnp.float32),
-            pltpu.VMEM((GROUP * rhs, wide), jnp.bfloat16),
-            pltpu.VMEM((GROUP * rhs, wide), jnp.float32),
-        ],
-        compiler_params=pltpu.CompilerParams(vmem_limit_bytes=48 * 2**20),
+            pltpu.VMEM((TOGETHER, GROUP * rhs, wide), jnp.bfloat16),
+            pltpu.VMEM((TOGETHER, GROUP * rhs, wide), jnp.float32),
+        ],
+        compiler_params=pltpu.CompilerParams(vmem_limit_bytes=MAIN_MIB * 2**20),
         cost_estimate=pl.CostEstimate(flops=8 * 10**9, bytes_accessed=32 * 2**20, transcendentals=0),
         name="image_and_terms",
     )(ids, own, earlier, oldest, turned)
-
-
-def prepare_kernel(x_ref, own_ref, late_ref, wide):
-    half, rhs, lanes = own_ref.shape
-    quarter = late_ref.shape[0]
-    depth = lanes // 2
-    for r in range(rhs):
-        turned = x_ref[:, r, :].T
-        wide[:, r, :] = jnp.concatenate([turned[:half], turned[half:]], axis=1)
-    own_ref[...] = wide[...].astype(jnp.bfloat16)
-    low = low_lanes((quarter, rhs, lanes))
-    first = pltpu.roll(wide[:quarter], depth, 2)
-    late_ref[...] = jnp.where(low, first, wide[quarter:]).astype(jnp.bfloat16)
-
-
-def prepare(right_side):
-    depth, rhs, blocks = right_side.shape
-    half = blocks // 2
-    return pl.pallas_call(
-        prepare_kernel,
-        out_shape=[
-            jax.ShapeDtypeStruct((half, rhs, 2 * depth), jnp.bfloat16),
-            jax.ShapeDtypeStruct((half // 2, rhs, 2 * depth), jnp.bfloat16),
-        ],
-        scratch_shapes=[pltpu.VMEM((half, rhs, 2 * depth), jnp.float32)],
-        compiler_params=pltpu.CompilerParams(vmem_limit_bytes=24 * 2**20),
-        name="prepare",
-    )(right_side)
 
 
 def finish_kernel(
@@ -233,12 +312,8 @@
     norms = jnp.sum(squares, axis=1, keepdims=True)
     part[...] = jnp.zeros_like(part)
     part[0:1, :] = jnp.sum(jnp.where(diagonal, norms, 0.0), axis=0, keepdims=True)
-    curves = jnp.sum(curve_ref[...], axis=0, keepdims=True)
-    curves = curves[:, :lanes] + curves[:, lanes:]
-    folded = curves
-    for turn in range(rhs, lanes, rhs):
-        folded = folded + pltpu.roll(curves, turn, 1)
-    part[1:2, :] = folded
+    curves = jnp.sum(curve_ref[...], axis=1, keepdims=True)
+    part[1:2, :] = jnp.sum(jnp.where(diagonal, curves, 0.0), axis=0, keepdims=True)
 
     pl.semaphore_wait(barrier, count - 1)
 
@@ -346,10 +421,7 @@
 
 
 def on_device(count, right_side, diag_tiles, off_tiles, neighbours):
-    own, late = prepare(right_side)
-    earlier = from_behind(own, "space", 1)
-    oldest = from_behind(late, "space", 2)
-    turned = turn_tiles(off_tiles, diag_tiles)
+    own, earlier, oldest, turned = turn_tiles(count, right_side, off_tiles, diag_tiles)
     for_oldest, for_earlier, own_sum, curve_parts = main_call(neighbours, own, earlier, oldest, turned)
     return tuple(finish(count, for_oldest, for_earlier, own_sum, curve_parts, right_side))
 

time: 81.5 us -> 67.3 us (0.83)
  Pallas kernels: 69.2 us -> 61.9 us
  starting transfers between devices: 6.81 us -> 0 us
    pallas_call x3 -> x2, Pallas kernels: 48.7 us -> 40.8 us  [the longest x1 22.5 us: main_call(): pl.pallas_call(main_kernel, grid=(groups // TOGETHER,), in_specs=[pl.Bloc...]
    ppermute x2 -> x0, starting transfers between devices: 6.81 us -> none  [from_behind(): lax.ppermute(value, axis, [(source, source + steps) for source in range(f...]
  transfers between devices with their start and end apart: 2 -> 0, of which waited for: 0 -> 0; matrix products, arithmetic and copies ran while one was open for 0% -> 0% of each run, Pallas kernels for 19% -> 0%
where the time goes in v3:
time: 67.3 us; the launch traced here: 67 us
  Pallas kernels  61.9 us (92%)
  local copies, waits for them, and re-layouts  4.4 us (7%)
  between operations  0.69 us (1%)
    pallas_call x1, Pallas kernels, main_call(): pl.pallas_call(main_kernel, grid=(groups // TOGETHER,), in_specs=[pl.Bloc...  22.5 us
    pallas_call x1, Pallas kernels, finish(): pl.pallas_call(functools.partial(finish_kernel, count), in_specs=[vmem] *...  21.1 us
    pallas_call x1, Pallas kernels, turn_tiles(): pl.pallas_call(functools.partial(turn_kernel, count), grid=(rows // step,...  18.3 us
    unnamed x10, local copies, waits for them, and re-layouts  4.4 us

profile of v3, /device:TPU:0, one launch (start us, length us, event | category | flops | bytes accessed | tf_op | source)
XLA Modules:
  0.0 67.0 jit_solution(11360641779145457026)
XLA Ops:
  0.6 0.0 copy-start
  0.6 1.2 %copy-done = f32[64,32,128]{2,1,0:T(8,128)S(1)} copy-done((f32[64,32,128]{2,1,0:T(8,128)S(1)}, f32[64,32,128]{2,1,0:T(8,128)}, u32[]{:S(2)}) %copy-start) | copy-done | bytes 1048600
  1.9 0.0 copy-start.2
  1.9 1.2 %copy-done.2 = bf16[64,64,128]{2,1,0:T(8,128)(2,1)S(1)} copy-done((bf16[64,64,128]{2,1,0:T(8,128)(2,1)S(1)}, bf16[64,64,128]{2,1,0:T(8,128)(2,1)}, u32[]{:S(2)}) %copy-start.2) | copy-done | bytes 1048600
  3.1 0.0 copy-start.3
  3.1 18.3 %turn_tiles.1 = (bf16[64,32,128]{2,1,0:T(8,128)(2,1)S(1)}, bf16[64,32,128]{2,1,0:T(8,128)(2,1)S(1)}, bf16[32,32,128]{2,1,0:T(8,128)(2,1)S(1)}, bf16[16,512,1024]{2,1,0:T(8,128)(2,1)}) custom-call(f32[64,32,128]{2,1,0:T(8,128)S(1)} %copy-done, bf16[15,64,64,128]{3,2,1,0:T(8,128)(2,1)} %off_ref.1, bf16[64,64,128]{2,1,0:T(8,128)(2,1)S(1)} %copy-done.2), custom_call_target="tpu_custom_call" | custom-call | tf_op jit(solution)/shard_map/turn_tiles/pallas_call | solution.py:120
  21.4 0.0 copy-start.1
  21.4 0.0 copy-done.3
  21.5 22.5 %image_and_terms.1 = (bf16[32,32,128]{2,1,0:T(8,128)(2,1)S(1)}, bf16[64,32,128]{2,1,0:T(8,128)(2,1)S(1)}, f32[64,32,128]{2,1,0:T(8,128)S(1)}, f32[32,128]{1,0:T(8,128)S(1)}) custom-call(s32[15,128]{1,0:T(8,128)S(1)} %copy-done.3, bf16[64,32,128]{2,1,0:T(8,128)(2,1)S(1)} %get-tuple-element.10.own_ref, bf16[64,32,128]{2,1,0:T(8,128)(2,1)S(1)} %get-tuple-element.11.earlier_ref, ...), custom_call_target="tpu_custom_call" | custom-call | flops 8000000000 | bytes 33554432 | tf_op jit(solution)/shard_map/image_and_terms/pallas_call | solution.py:257
  44.0 0.0 copy-done.1
  44.0 21.1 %finish.1 = (f32[64,32,128]{2,1,0:T(8,128)S(1)}, f32[64,32,128]{2,1,0:T(8,128)S(1)}) custom-call(bf16[32,32,128]{2,1,0:T(8,128)(2,1)S(1)} %get-tuple-element.14.oldest_ref, bf16[64,32,128]{2,1,0:T(8,128)(2,1)S(1)} %get-tuple-element.15.earlier_ref, f32[64,32,128]{2,1,0:T(8,128)S(1)} %get-tuple-element.16.own_ref, f32[32,128]{1,0:T(8,128)S(1)} %get-tuple-element.17.curve_ref, ...), custom_call_target="tpu_custom_call" | custom-call | tf_op jit(solution)/shard_map/finish/pallas_call | solution.py:400
  65.0 1.0 %copy.8 = f32[64,32,128]{2,1,0:T(8,128)} copy(f32[64,32,128]{2,1,0:T(8,128)S(1)} %get-tuple-element.20) | data formatting | bytes 2097152
  66.0 1.0 %copy.9 = f32[64,32,128]{2,1,0:T(8,128)} copy(f32[64,32,128]{2,1,0:T(8,128)S(1)} %get-tuple-element.21) | data formatting | bytes 2097152
Async XLA Ops:
  0.6 1.2 %copy-start = (f32[64,32,128]{2,1,0:T(8,128)S(1)}, f32[64,32,128]{2,1,0:T(8,128)}, u32[]{:S(2)}) copy-start(f32[64,32,128]{2,1,0:T(8,128)} %x_ref.3) | copy-start | bytes 3145732
  1.9 1.2 %copy-start.2 = (bf16[64,64,128]{2,1,0:T(8,128)(2,1)S(1)}, bf16[64,64,128]{2,1,0:T(8,128)(2,1)}, u32[]{:S(2)}) copy-start(bf16[64,64,128]{2,1,0:T(8,128)(2,1)} %diag_ref.1) | copy-start | bytes 3145732
  3.1 18.4 %copy-start.3 = (s32[15,128]{1,0:T(8,128)S(1)}, s32[15,128]{1,0:T(8,128)}, u32[]{:S(2)}) copy-start(s32[15,128]{1,0:T(8,128)} %ids_ref.1) | copy-start | bytes 23044
  21.4 22.5 %copy-start.1 = (f32[64,32,128]{2,1,0:T(8,128)S(1)}, f32[64,32,128]{2,1,0:T(8,128)}, u32[]{:S(2)}) copy-start(f32[64,32,128]{2,1,0:T(8,128)} %x_ref.3) | copy-start | bytes 3145732
